TPU v7x, 128 devices: a whole 4x4x4 slice. The times are simulated.
128 devices in a mesh: row: 16 (over y_lo, z, core), col: 8 (over y_hi, x).
Axes of the slice: x: 4, y: 4 (y_hi: 2, y_lo: 2; y = y_hi * 2 + y_lo), z: 4, core: 2. Of those that a mesh axis runs over, the one named last changes fastest.
Arguments:
- tokens: bfloat16 [1024, 6144], P('col', 'row'), may hold values from -6 to 6
- weight_in: bfloat16 [6144, 24576], P('row', 'col'), may hold values from -0.078125 to 0.078125
- weight_out: bfloat16 [24576, 6144], P('col', 'row'), may hold values from -0.078125 to 0.078125
- upstream: bfloat16 [1024, 6144], P('col', 'row'), may hold values from -6 to 6
Outputs:
- grad_tokens: bfloat16 [1024, 6144], P('col', 'row')
- grad_in: bfloat16 [6144, 24576], P('row', 'col')
- grad_out: bfloat16 [24576, 6144], P('col', 'row')
All inputs are finite; a program needn't handle non-finite values.
Results may differ from a plain program's by a relative error of at most 0.005.
Values may be sent and summed in bfloat16 or wider, within the bound.
A program may use at most 128 MiB of HBM per device.

v0:
```python
import jax
import jax.numpy as jnp
from jax import lax
from jax.sharding import PartitionSpec as P

coef = 0.7978845608
cubic = 0.044715


def activate(hidden, back):
    inner = coef * (hidden + cubic * hidden * hidden * hidden)
    tangent = jnp.tanh(inner)
    value = 0.5 * hidden * (1.0 + tangent)
    slope = 0.5 * (1.0 + tangent) + 0.5 * hidden * (1.0 - tangent * tangent) * coef * (
        1.0 + 3.0 * cubic * hidden * hidden
    )
    return (value.astype(jnp.bfloat16), (back * slope).astype(jnp.bfloat16))


def contract_last(left, right):
    return lax.dot_general(
        left, right, (((1,), (1,)), ((), ())), preferred_element_type=jnp.float32
    )


def contract_first(left, right):
    return lax.dot_general(
        left, right, (((0,), (0,)), ((), ())), preferred_element_type=jnp.float32
    )


def shards(tokens, weight_in, weight_out, upstream):
    tok_all, cot_all = (
        lax.all_gather(tokens, "col", axis=0, tiled=True),
        lax.all_gather(upstream, "col", axis=0, tiled=True),
    )
    width_hid = weight_in.shape[1]
    sums = lax.psum_scatter(
        jnp.concatenate(
            [
                jnp.dot(tok_all, weight_in, preferred_element_type=jnp.float32),
                contract_last(cot_all, weight_out),
            ],
            axis=1,
        ),
        "row",
        scatter_dimension=0,
        tiled=True,
    )
    hidden_local = sums[:, :width_hid]
    back_local = sums[:, width_hid:]
    act_local, grad_local = activate(hidden_local, back_local)
    act_all, grad_all = (
        lax.all_gather(act_local, "row", axis=0, tiled=True),
        lax.all_gather(grad_local, "row", axis=0, tiled=True),
    )
    grad_in = contract_first(tok_all, grad_all).astype(jnp.bfloat16)
    grad_out = contract_first(act_all, cot_all).astype(jnp.bfloat16)
    grad_tokens = lax.psum_scatter(
        contract_last(grad_all, weight_in), "col", scatter_dimension=0, tiled=True
    ).astype(jnp.bfloat16)
    return (grad_tokens, grad_in, grad_out)


def solution(mesh):
    placed = (P("col", "row"), P("row", "col"), P("col", "row"), P("col", "row"))
    return jax.shard_map(
        shards,
        mesh=mesh,
        in_specs=placed,
        out_specs=(P("col", "row"), P("row", "col"), P("col", "row")),
        check_vma=False,
    )
```

profile of v0, /device:TPU:0, one launch (start us, length us, event | category | flops | bytes accessed | tf_op | source)
XLA Modules:
  0.0 416.0 jit_solution(14746245070475281897)
XLA Ops:
  7.2 0.0 copy-start
  7.2 0.0 reduce-scatter.3.cloned.1.call-start
  7.2 36.7 %all_gather.12 = bf16[1024,384]{1,0:T(8,128)(2,1)S(1)} all-gather(bf16[128,384]{1,0:T(8,128)(2,1)} %param.4), channel_id=1, replica_groups=mesh['row'=16,'col'=8] {'col'}, dimensions={0}, use_global_device_ids=true | all-gather | bytes 884736 | tf_op jit(solution)/shard_map/all_gather | solution.py:34
  43.9 35.8 %all_gather.13 = bf16[1024,384]{1,0:T(8,128)(2,1)S(1)} all-gather(bf16[128,384]{1,0:T(8,128)(2,1)} %param.7), channel_id=1, replica_groups=mesh['row'=16,'col'=8] {'col'}, dimensions={0}, use_global_device_ids=true | all-gather | bytes 884736 | tf_op jit(solution)/shard_map/all_gather | solution.py:35
  79.7 0.0 copy-start.1
  79.7 5.4 %fusion.9 = f32[1024,3072]{1,0:T(8,128)S(1)} fusion(bf16[1024,384]{1,0:T(8,128)(2,1)S(1)} %all_gather.13, bf16[3072,384]{1,0:T(8,128)(2,1)} %param.6), kind=kOutput, calls=%fused_computation.15 | convolution fusion | flops 2415919104 | bytes 15728640 | tf_op jit(solution)/shard_map/dot_general | solution.py:21
  85.2 0.0 copy-done.1
  85.2 0.0 copy-done
  85.2 3.4 fusion.8
  88.6 8.7 %pad_maximum_fusion = f32[1024,6144]{1,0:T(8,128)} fusion(f32[1024,3072]{1,0:T(8,128)S(1)} %fusion.9, f32[1024,3072]{1,0:T(8,128)S(1)} %fusion.8), kind=kLoop, calls=%fused_computation | loop fusion | flops 6291456 | bytes 50331648 | tf_op jit(solution)/shard_map/concatenate | solution.py:39
  97.3 0.0 reduce-scatter.3.cloned.1.call-update
  97.4 0.0 all-gather.3.cloned.1.call-start
  97.4 142.9 %reduce-scatter.3.cloned.1.call-done = f32[64,6144]{1,0:T(8,128)} async-done(((f32[1024,6144]{1,0:T(8,128)}), f32[64,6144]{1,0:T(8,128)}) %reduce-scatter.3.cloned.1.call-update) | async-done | bytes 1572880 | tf_op jit(solution)/shard_map/reduce_scatter | solution.py:38
  240.3 2.8 multiply_convert_fusion
  243.0 0.0 all-gather.3.cloned.1.call-update
  243.1 0.0 all-gather.5.cloned.1.call-start
  243.1 0.7 all-gather.5.cloned.1.call-update
  243.8 0.2 reduce-scatter.5.cloned.1.call-start
  244.0 40.1 %all-gather.3.cloned.1.call-done = bf16[1024,3072]{1,0:T(8,128)(2,1)} async-done(((bf16[64,3072]{1,0:T(8,128)(2,1)}), bf16[1024,3072]{1,0:T(8,128)(2,1)}) %all-gather.3.cloned.1.call-update) | async-done | bytes 6291472 | tf_op jit(solution)/shard_map/all_gather | solution.py:55
  284.2 6.7 %fusion.10 = f32[1024,384]{1,0:T(8,128)} fusion(bf16[1024,3072]{1,0:T(8,128)(2,1)} %all-gather.3.cloned.1.call-done, bf16[384,3072]{1,0:T(8,128)(2,1)S(1)} %copy-done), kind=kOutput, calls=%fused_computation.16 | convolution fusion | flops 2415919104 | bytes 10223616 | tf_op jit(solution)/shard_map/dot_general | solution.py:21
  290.8 0.0 reduce-scatter.5.cloned.1.call-update
  290.9 7.7 %fusion = bf16[384,3072]{0,1:T(8,128)(2,1)} fusion(bf16[1024,3072]{1,0:T(8,128)(2,1)} %all-gather.3.cloned.1.call-done, bf16[1024,384]{1,0:T(8,128)(2,1)S(1)} %all_gather.12), kind=kOutput, calls=%fused_computation.3 | convolution fusion | flops 2417098752 | bytes 9437184 | tf_op jit(solution)/shard_map/dot_general | solution.py:27
  298.5 0.0 copy-start.2
  298.5 4.3 %copy.7 = bf16[384,3072]{1,0:T(8,128)(2,1)} copy(bf16[384,3072]{0,1:T(8,128)(2,1)} %fusion) | data formatting | bytes 4718592
  302.9 26.3 %all-gather.5.cloned.1.call-done = bf16[1024,3072]{1,0:T(8,128)(2,1)} async-done(((bf16[64,3072]{1,0:T(8,128)(2,1)}), bf16[1024,3072]{1,0:T(8,128)(2,1)}) %all-gather.5.cloned.1.call-update) | async-done | bytes 6291472 | tf_op jit(solution)/shard_map/all_gather | solution.py:54
  329.2 0.0 copy-done.2
  329.2 7.7 %convolution_convert_fusion = bf16[3072,384]{1,0:T(8,128)(2,1)} fusion(bf16[1024,3072]{1,0:T(8,128)(2,1)} %all-gather.5.cloned.1.call-done, bf16[1024,384]{1,0:T(8,128)(2,1)S(1)} %copy-done.2), kind=kOutput, calls=%fused_computation.1 | convolution fusion | flops 2417098752 | bytes 9437184 | tf_op jit(solution)/shard_map/dot_general | solution.py:27
  336.8 71.0 %reduce-scatter.5.cloned.1.call-done = f32[128,384]{1,0:T(8,128)} async-done(((f32[1024,384]{1,0:T(8,128)}), f32[128,384]{1,0:T(8,128)}) %reduce-scatter.5.cloned.1.call-update) | async-done | bytes 196624 | tf_op jit(solution)/shard_map/reduce_scatter | solution.py:59
  407.9 1.6 convert_element_type.19
Async XLA Ops:
  7.2 78.0 %copy-start = (bf16[384,3072]{1,0:T(8,128)(2,1)S(1)}, bf16[384,3072]{1,0:T(8,128)(2,1)}, u32[]{:S(2)}) copy-start(bf16[384,3072]{1,0:T(8,128)(2,1)} %param.5) | copy-start | bytes 7077892
  7.2 233.1 %reduce-scatter.3.cloned.1.call-start = ((), (), s32[]{:S(2)}) async-start(), calls=%async_computation.2 | async-start | bytes 26738688 | tf_op jit(solution)/shard_map/reduce_scatter | solution.py:38
  79.7 5.4 %copy-start.1 = (bf16[1024,384]{1,0:T(8,128)(2,1)}, bf16[1024,384]{1,0:T(8,128)(2,1)S(1)}, u32[]{:S(2)}) copy-start(bf16[1024,384]{1,0:T(8,128)(2,1)S(1)} %all_gather.13) | copy-start | bytes 2359300
  97.4 186.8 %all-gather.3.cloned.1.call-start = ((), (), s32[]{:S(2)}) async-start(), calls=%async_computation.3 | async-start | bytes 6684672 | tf_op jit(solution)/shard_map/all_gather | solution.py:55
  243.1 86.1 %all-gather.5.cloned.1.call-start = ((), (), s32[]{:S(2)}) async-start(), calls=%async_computation.5 | async-start | bytes 6684672 | tf_op jit(solution)/shard_map/all_gather | solution.py:54
  243.8 164.1 %reduce-scatter.5.cloned.1.call-start = ((), (), s32[]{:S(2)}) async-start(), calls=%async_computation.4 | async-start | bytes 1769472 | tf_op jit(solution)/shard_map/reduce_scatter | solution.py:59
  298.5 30.6 %copy-start.2 = (bf16[1024,384]{1,0:T(8,128)(2,1)S(1)}, bf16[1024,384]{1,0:T(8,128)(2,1)}, u32[]{:S(2)}) copy-start(bf16[1024,384]{1,0:T(8,128)(2,1)} %copy-done.1) | copy-start | bytes 2359300
Sparse Core Ops, SparseCore 0:
  97.5 142.7 reduce-scatter.2
  243.2 40.9 all-gather.2
  285.9 43.2 all-gather.4
  332.8 75.0 reduce-scatter.4
where the time goes:
time: 416 us
  waiting for transfers between devices  281 us (68%)
  blocking collectives  72.5 us (17%)
  matrix products  30.9 us (7%)
  between operations  13.8 us (3%)
  other arithmetic  13.1 us (3%)
  local copies, waits for them, and re-layouts  4.37 us (1%)
    reduce_scatter x1, waiting for transfers between devices, shards(): lax.psum_scatter(jnp.concatenate([jnp.dot(tok_all, weight_in, preferred_e...  143 us
    reduce_scatter x1, waiting for transfers between devices, shards(): lax.psum_scatter(contract_last(grad_all, weight_in), 'col', scatter_dimen...  71 us
    all_gather x1, waiting for transfers between devices, shards(): lax.all_gather(grad_local, 'row', axis=0, tiled=True)  40.1 us
    all_gather x1, blocking collectives, shards(): lax.all_gather(tokens, 'col', axis=0, tiled=True)  36.7 us
    all_gather x1, blocking collectives, shards(): lax.all_gather(upstream, 'col', axis=0, tiled=True)  35.8 us
    all_gather x1, waiting for transfers between devices, shards(): lax.all_gather(act_local, 'row', axis=0, tiled=True)  26.3 us
    dot_general x2, matrix products, contract_first(): lax.dot_general(left, right, (((0,), (0,)), ((), ())), preferred_element_...  15.3 us
    dot_general x2, matrix products, contract_last(): lax.dot_general(left, right, (((1,), (1,)), ((), ())), preferred_element_...  12.1 us
  transfers between devices with their start and end apart: 4, of which 4 were waited for; matrix products, arithmetic and copies ran while one was open for 6% of the time, Pallas kernels for 0%

commit v1 on v0

--- a/solution.py
+++ b/solution.py
@@ -51,7 +51,9 @@
     back_local = sums[:, width_hid:]
     act_local, grad_local = activate(hidden_local, back_local)
     act_all, grad_all = (
-        lax.all_gather(act_local, "row", axis=0, tiled=True),
+        jnp.concatenate(
+            lax.all_to_all(jnp.stack([act_local] * lax.axis_size("row")), "row", 0, 0), axis=0
+        ),
         lax.all_gather(grad_local, "row", axis=0, tiled=True),
     )
     grad_in = contract_first(tok_all, grad_all).astype(jnp.bfloat16)

time: 416 us -> 454 us (1.091)
  waiting for transfers between devices: 281 us -> 310 us
  starting transfers between devices: 0.34 us -> 4.93 us
    all_gather x1, waiting for transfers between devices: 40.1 us -> 103 us  [shards(): lax.all_gather(grad_local, 'row', axis=0, tiled=True)]
    all_gather x1 -> x0, waiting for transfers between devices: 26.3 us -> none  [shards(): lax.all_gather(act_local, 'row', axis=0, tiled=True)]
    reduce_scatter x1, waiting for transfers between devices: 71 us -> 62.7 us  [shards(): lax.psum_scatter(contract_last(grad_all, weight_in), 'col', scatter_dimen...]
    all_to_all x0 -> x1, starting transfers between devices: none -> 4.63 us  [shards(): lax.all_to_all(jnp.stack([act_local] * lax.axis_size('row')), 'row', 0, 0)]
  transfers between devices with their start and end apart: 4 -> 4, of which waited for: 4 -> 4; matrix products, arithmetic and copies ran while one was open for 6% -> 7% of each run, Pallas kernels for 0% -> 0%
where the time goes in v1:
time: 454 us; the launch traced here: 453 us
  waiting for transfers between devices  310 us (68%)
  blocking collectives  72.5 us (16%)
  matrix products  30.8 us (7%)
  between operations  13.8 us (3%)
  other arithmetic  13 us (3%)
  local copies, waits for them, and re-layouts  8.56 us (2%)
  starting transfers between devices  4.93 us (1%)
    reduce_scatter x1, waiting for transfers between devices, shards(): lax.psum_scatter(jnp.concatenate([jnp.dot(tok_all, weight_in, preferred_e...  143 us
    all_gather x1, waiting for transfers between devices, shards(): lax.all_gather(grad_local, 'row', axis=0, tiled=True)  103 us
    reduce_scatter x1, waiting for transfers between devices, shards(): lax.psum_scatter(contract_last(grad_all, weight_in), 'col', scatter_dimen...  62.7 us
    all_gather x1, blocking collectives, shards(): lax.all_gather(tokens, 'col', axis=0, tiled=True)  36.7 us
    all_gather x1, blocking collectives, shards(): lax.all_gather(upstream, 'col', axis=0, tiled=True)  35.8 us
    dot_general x2, matrix products, contract_first(): lax.dot_general(left, right, (((0,), (0,)), ((), ())), preferred_element_...  15.5 us
    dot_general x2, matrix products, contract_last(): lax.dot_general(left, right, (((1,), (1,)), ((), ())), preferred_element_...  11.8 us
  transfers between devices with their start and end apart: 4, of which 4 were waited for; matrix products, arithmetic and copies ran while one was open for 7% of the time, Pallas kernels for 0%

profile of v1, /device:TPU:0, one launch (start us, length us, event | category | flops | bytes accessed | tf_op | source)
XLA Modules:
  0.0 453.1 jit_solution(4543105276841453667)
XLA Ops:
  7.2 0.0 copy-start
  7.2 0.0 reduce-scatter.3.cloned.1.call-start
  7.2 36.7 %all_gather.9 = bf16[1024,384]{1,0:T(8,128)(2,1)S(1)} all-gather(bf16[128,384]{1,0:T(8,128)(2,1)} %param.4), channel_id=1, replica_groups=mesh['row'=16,'col'=8] {'col'}, dimensions={0}, use_global_device_ids=true | all-gather | bytes 884736 | tf_op jit(solution)/shard_map/all_gather | solution.py:34
  43.9 35.8 %all_gather.10 = bf16[1024,384]{1,0:T(8,128)(2,1)S(1)} all-gather(bf16[128,384]{1,0:T(8,128)(2,1)} %param.7), channel_id=1, replica_groups=mesh['row'=16,'col'=8] {'col'}, dimensions={0}, use_global_device_ids=true | all-gather | bytes 884736 | tf_op jit(solution)/shard_map/all_gather | solution.py:35
  79.7 0.0 copy-start.1
  79.7 0.9 copy-done.1
  80.6 5.1 %fusion.9 = f32[1024,3072]{1,0:T(8,128)S(1)} fusion(bf16[1024,384]{1,0:T(8,128)(2,1)S(1)} %all_gather.10, bf16[3072,384]{1,0:T(8,128)(2,1)} %param.6), kind=kOutput, calls=%fused_computation.15 | convolution fusion | flops 2415919104 | bytes 15728640 | tf_op jit(solution)/shard_map/dot_general | solution.py:21
  85.8 0.0 copy-done
  85.8 3.4 fusion.8
  89.2 8.7 %pad_maximum_fusion = f32[1024,6144]{1,0:T(8,128)} fusion(f32[1024,3072]{1,0:T(8,128)S(1)} %fusion.9, f32[1024,3072]{1,0:T(8,128)S(1)} %fusion.8), kind=kLoop, calls=%fused_computation | loop fusion | flops 6291456 | bytes 50331648 | tf_op jit(solution)/shard_map/concatenate | solution.py:39
  97.9 0.0 reduce-scatter.3.cloned.1.call-update
  98.0 0.0 all-gather.2.cloned.1.call-start
  98.0 142.8 %reduce-scatter.3.cloned.1.call-done = f32[64,6144]{1,0:T(8,128)} async-done(((f32[1024,6144]{1,0:T(8,128)}), f32[64,6144]{1,0:T(8,128)}) %reduce-scatter.3.cloned.1.call-update) | async-done | bytes 1572880 | tf_op jit(solution)/shard_map/reduce_scatter | solution.py:38
  240.8 2.7 multiply_convert_fusion
  243.5 0.0 all-gather.2.cloned.1.call-update
  243.5 3.4 stack.2
  246.9 4.6 %all-to-all-start = ((bf16[16,64,3072]{2,1,0:T(8,128)(2,1)}), bf16[16,64,3072]{2,1,0:T(8,128)(2,1)}, u32[]{:S(2)}, u32[]{:S(2)}) async-start(bf16[16,64,3072]{2,1,0:T(8,128)(2,1)} %stack.2), calls=%async_computation.2 | async-start | bytes 12582912 | tf_op jit(solution)/shard_map/all_to_all | solution.py:55
  251.5 0.2 reduce-scatter.5.cloned.1.call-start
  251.8 102.9 %all-gather.2.cloned.1.call-done = bf16[1024,3072]{1,0:T(8,128)(2,1)} async-done(((bf16[64,3072]{1,0:T(8,128)(2,1)}), bf16[1024,3072]{1,0:T(8,128)(2,1)}) %all-gather.2.cloned.1.call-update) | async-done | bytes 6291472 | tf_op jit(solution)/shard_map/all_gather | solution.py:57
  354.6 6.7 %fusion.10 = f32[1024,384]{1,0:T(8,128)} fusion(bf16[1024,3072]{1,0:T(8,128)(2,1)} %all-gather.2.cloned.1.call-done, bf16[384,3072]{1,0:T(8,128)(2,1)S(1)} %copy-done), kind=kOutput, calls=%fused_computation.16 | convolution fusion | flops 2415919104 | bytes 10223616 | tf_op jit(solution)/shard_map/dot_general | solution.py:21
  361.3 0.0 reduce-scatter.5.cloned.1.call-update
  361.3 1.2 all-to-all-done
  362.5 7.8 %convolution_convert_fusion = bf16[3072,384]{1,0:T(8,128)(2,1)} fusion(bf16[1024,3072]{1,0:T(8,128)(2,1)} %bitcast.1, bf16[1024,384]{1,0:T(8,128)(2,1)} %copy-done.1), kind=kOutput, calls=%fused_computation.1 | convolution fusion | flops 2417098752 | bytes 9437184 | tf_op jit(solution)/shard_map/dot_general | solution.py:27
  370.4 7.7 %fusion = bf16[384,3072]{0,1:T(8,128)(2,1)} fusion(bf16[1024,3072]{1,0:T(8,128)(2,1)} %all-gather.2.cloned.1.call-done, bf16[1024,384]{1,0:T(8,128)(2,1)S(1)} %all_gather.9), kind=kOutput, calls=%fused_computation.3 | convolution fusion | flops 2417098752 | bytes 9437184 | tf_op jit(solution)/shard_map/dot_general | solution.py:27
  378.1 4.3 copy.7
  382.4 62.7 %reduce-scatter.5.cloned.1.call-done = f32[128,384]{1,0:T(8,128)} async-done(((f32[1024,384]{1,0:T(8,128)}), f32[128,384]{1,0:T(8,128)}) %reduce-scatter.5.cloned.1.call-update) | async-done | bytes 196624 | tf_op jit(solution)/shard_map/reduce_scatter | solution.py:61
  445.0 1.6 convert_element_type.19
Async XLA Ops:
  7.2 78.6 %copy-start = (bf16[384,3072]{1,0:T(8,128)(2,1)S(1)}, bf16[384,3072]{1,0:T(8,128)(2,1)}, u32[]{:S(2)}) copy-start(bf16[384,3072]{1,0:T(8,128)(2,1)} %param.5) | copy-start | bytes 7077892
  7.2 233.7 %reduce-scatter.3.cloned.1.call-start = ((), (), s32[]{:S(2)}) async-start(), calls=%async_computation.3 | async-start | bytes 26738688 | tf_op jit(solution)/shard_map/reduce_scatter | solution.py:38
  79.7 0.9 copy-start.1
  98.0 256.7 %all-gather.2.cloned.1.call-start = ((), (), s32[]{:S(2)}) async-start(), calls=%async_computation.4 | async-start | bytes 6684672 | tf_op jit(solution)/shard_map/all_gather | solution.py:57
  246.9 115.6 %all-to-all-start = ((bf16[16,64,3072]{2,1,0:T(8,128)(2,1)}), bf16[16,64,3072]{2,1,0:T(8,128)(2,1)}, u32[]{:S(2)}, u32[]{:S(2)}) async-start(bf16[16,64,3072]{2,1,0:T(8,128)(2,1)} %stack.2), calls=%async_computation.2 | async-start | bytes 12582912 | tf_op jit(solution)/shard_map/all_to_all | solution.py:55
  251.5 193.5 %reduce-scatter.5.cloned.1.call-start = ((), (), s32[]{:S(2)}) async-start(), calls=%async_computation.5 | async-start | bytes 1769472 | tf_op jit(solution)/shard_map/reduce_scatter | solution.py:61
Sparse Core Ops, SparseCore 0:
  98.1 142.7 reduce-scatter.2
  243.6 110.9 all-gather.1
  361.4 83.5 reduce-scatter.4
